TPU v7x, 512 devices: a whole 4x8x8 slice. The times are simulated.
512 devices in a mesh: land: 8 (over x, z_hi), dp: 64 (over z_lo, y, core).
Axes of the slice: x: 4, y: 8, z: 8 (z_hi: 2, z_lo: 4; z = z_hi * 4 + z_lo), core: 2. Of those that a mesh axis runs over, the one named last changes fastest.
Arguments:
- embeddings: bfloat16 [32768, 1280], P(('dp', 'land')), may hold values from -6 to 6
- landmarks: bfloat16 [8192, 1280], P(('land', 'dp')), may hold values from -6 to 6
- factor: bfloat16 [8192, 1024], P(('land', 'dp')), may hold values from -6 to 6
- centroids: bfloat16 [4096, 1024], P('land'), may hold values from -6 to 6
- assignment: int32 [32768], P('dp'), may hold values from 0 to 4095, as said below
Outputs:
- distances: float32 [32768, 4096], P('dp', 'land')
- new_centroids: float32 [4096, 1024], P(('land', 'dp'))
Inputs may be any that keep to these rules, and one draw needn't show every extreme that they name: `assignment`: among the 512 rows of one index of dp, at most 2 are assigned to centroids of any one aligned block of 8 centroid numbers.
All inputs are finite; a program needn't handle non-finite values.
Results may differ from a plain program's by a relative error of at most 0.01.
Values may be sent and summed in bfloat16 or wider, within the bound.
A program may use at most 64 MiB of HBM per device.

v0:
```python
import math

import jax
import jax.numpy as jnp
from jax import lax
from jax.sharding import PartitionSpec as P

EPSILON = 1e-06
SHARPNESS = 6.0


def in_order(parts, dim):
    parts = jnp.moveaxis(parts, 0, dim)
    dims = parts.shape
    return parts.reshape(*dims[:dim], dims[dim] * dims[dim + 1], *dims[dim + 2 :])


def copy_for_each(shard, axis):
    devices = lax.axis_size(axis)
    return lax.all_to_all(
        jnp.broadcast_to(shard[None], (devices, *shard.shape)), axis, 0, 0, tiled=True
    )


def gather_directly(shard, axis, dim):
    return in_order(copy_for_each(shard, axis), dim)


def sent_together(arrays, axis, dim, along):
    widths = [a.shape[along] for a in arrays]
    both = jnp.concatenate(arrays, axis=along)
    whole = lax.all_gather(both, axis, axis=dim, tiled=True)
    return tuple(jnp.split(whole, [sum(widths[:k]) for k in range(1, len(widths))], axis=along))


def in_one_piece(arrays, axis, split_dim, concat_dim, along):
    widths = [math.prod(a.shape[along:]) for a in arrays]
    both = jnp.concatenate(
        [a.reshape(*a.shape[:along], w) for a, w in zip(arrays, widths)], axis=along
    )
    whole = lax.all_to_all(both, axis, split_axis=split_dim, concat_axis=concat_dim, tiled=True)
    parts = jnp.split(whole, [sum(widths[:k]) for k in range(1, len(widths))], axis=along)
    return tuple((b.reshape(*whole.shape[:along], *a.shape[along:]) for a, b in zip(arrays, parts)))


def local(embeddings, landmarks, factor, centroids, assignment):
    group_rows = gather_directly(embeddings, "land", 0)
    embed_width = group_rows.shape[1]
    feat_width = factor.shape[1]
    row_scale = lax.rsqrt(jnp.mean(jnp.square(group_rows.astype(jnp.float32)), axis=1) + EPSILON)
    row_coef = row_scale / embed_width
    mark_rows, factor_part = sent_together((landmarks, factor), "dp", 0, 1)
    mark_scale = lax.rsqrt(jnp.mean(jnp.square(mark_rows.astype(jnp.float32)), axis=1) + EPSILON)
    inner_dots = lax.dot_general(
        group_rows, mark_rows, (((1,), (1,)), ((), ())), preferred_element_type=jnp.float32
    )
    similarity = inner_dots * row_coef[:, None] * mark_scale[None, :]
    partial_value = jnp.dot(
        jnp.exp(SHARPNESS * (similarity - 1.0)).astype(jnp.bfloat16),
        factor_part,
        preferred_element_type=jnp.float32,
    )
    features = lax.psum(partial_value.astype(jnp.bfloat16), "land")
    feat_sq = jnp.sum(jnp.square(features.astype(jnp.float32)), axis=1)
    cent_sq = jnp.sum(jnp.square(centroids.astype(jnp.float32)), axis=1)
    cross_term = lax.dot_general(
        features, centroids, (((1,), (1,)), ((), ())), preferred_element_type=jnp.float32
    )
    distances = (feat_sq[:, None] + cent_sq[None, :] - 2.0 * cross_term) / feat_width
    cent_block = centroids.shape[0]
    land_count = lax.axis_size("land")
    dp_count = lax.axis_size("dp")
    row_total = features.shape[0]
    own_width = cent_block // dp_count
    slot_count = 2 * max(1, row_total // (land_count * dp_count))
    slice_id = assignment // own_width
    target_land = slice_id // dp_count
    target_dp = slice_id % dp_count
    local_id = assignment % own_width
    in_block = target_land == lax.axis_index("land")
    row_pos = lax.iota(jnp.int32, row_total)
    earlier = (
        (target_dp[None, :] == target_dp[:, None])
        & in_block[None, :]
        & (row_pos[None, :] < row_pos[:, None])
    )
    slot_rank = jnp.sum(earlier.astype(jnp.int32), axis=1)
    slot_of = jnp.where(in_block, target_dp * slot_count + slot_rank, -1)
    slot_pos = lax.iota(jnp.int32, dp_count * slot_count)
    slot_pick = slot_pos[:, None] == slot_of[None, :]
    outgoing = jnp.dot(
        slot_pick.astype(jnp.bfloat16), features, preferred_element_type=jnp.float32
    ).astype(jnp.bfloat16)
    slot_ids = (
        jnp.max(jnp.where(slot_pick, local_id[None, :], -1), axis=1)
        .astype(jnp.float32)
        .astype(jnp.bfloat16)
    )
    outgoing = outgoing.reshape(dp_count, slot_count, feat_width)
    slot_ids = slot_ids.reshape(dp_count, slot_count)
    arrived, arrived_ids = in_one_piece((outgoing, slot_ids), "dp", 0, 0, 2)
    arrived = arrived.reshape(dp_count * slot_count, feat_width)
    arrived_ids = arrived_ids.reshape(dp_count * slot_count).astype(jnp.float32)
    id_match = arrived_ids[None, :] == lax.iota(jnp.float32, own_width)[:, None]
    cent_sums = jnp.dot(id_match.astype(jnp.bfloat16), arrived, preferred_element_type=jnp.float32)
    cent_counts = jnp.sum(id_match.astype(jnp.float32), axis=1)
    new_centroids = cent_sums / jnp.maximum(cent_counts, 1.0)[:, None]
    return (distances, new_centroids)


def solution(mesh):
    return jax.shard_map(
        local,
        mesh=mesh,
        in_specs=(
            P(("dp", "land"), None),
            P(("land", "dp"), None),
            P(("land", "dp"), None),
            P("land", None),
            P("dp"),
        ),
        out_specs=(P("dp", "land"), P(("land", "dp"), None)),
        check_vma=False,
    )
```

profile of v0, /device:TPU:1, one launch (start us, length us, event | category | flops | bytes accessed | tf_op | source)
XLA Modules:
  0.0 334.6 jit_solution(3606833546896402082)
XLA Ops:
  7.2 0.0 all-gather.2.cloned.1.call-start
  7.2 1.4 pad_maximum_fusion.1
  8.6 0.0 all-gather.2.cloned.1.call-update
  8.7 2.1 broadcast_in_dim.11
  10.8 13.3 %all-to-all-start = ((bf16[8,64,1280]{2,1,0:T(8,128)(2,1)}), bf16[8,64,1280]{2,1,0:T(8,128)(2,1)S(1)}, u32[]{:S(2)}, u32[]{:S(2)}) async-start(bf16[8,64,1280]{2,1,0:T(8,128)(2,1)} %broadcast_in_dim.11), calls=%async_computation | async-start | bytes 2621440 | tf_op jit(solution)/shard_map/all_to_all | solution.py:20
  24.1 0.0 all-reduce.2.cloned.1.call-start
  24.1 25.7 %all-to-all-done = bf16[8,64,1280]{2,1,0:T(8,128)(2,1)S(1)} async-done(((bf16[8,64,1280]{2,1,0:T(8,128)(2,1)}), bf16[8,64,1280]{2,1,0:T(8,128)(2,1)S(1)}, u32[]{:S(2)}, u32[]{:S(2)}) %all-to-all-start) | async-done | bytes 1310752 | tf_op jit(solution)/shard_map/all_to_all | solution.py:20
  49.8 0.3 multiply_reduce_fusion.1
  50.2 0.1 div.52
  50.3 102.2 %all-gather.2.cloned.1.call-done = bf16[1024,2304]{1,0:T(8,128)(2,1)} async-done(((bf16[16,2304]{1,0:T(8,128)(2,1)}), bf16[1024,2304]{1,0:T(8,128)(2,1)}) %all-gather.2.cloned.1.call-update) | async-done | bytes 4718608 | tf_op jit(solution)/shard_map/all_gather | solution.py:32
  152.5 2.3 multiply_reduce_fusion
  154.8 0.0 copy-start.2
  154.8 6.3 %fusion.6 = bf16[512,1024]{1,0:T(8,128)(2,1)} fusion(bf16[1024,2304]{1,0:T(8,128)(2,1)} %all-gather.2.cloned.1.call-done, bf16[512,1280]{1,0:T(8,128)(2,1)S(1)} %bitcast.6, f32[1024]{0:T(1024)S(1)} %add_rsqrt_fusion, f32[512]{0:T(512)S(1)} %div.52), kind=kOutput, calls=%fused_computation.9 | convolution fusion | flops 2419064832 | bytes 7084032 | tf_op jit(solution)/shard_map/dot_general | solution.py:58
  161.1 0.0 copy-start.1
  161.1 0.0 all-reduce.2.cloned.1.call-update
  161.2 0.0 copy-done.2
  161.2 0.3 convert_reduce_fusion
  161.5 0.1 select_reduce_fusion
  161.6 0.2 convert_element_type.80
  161.9 135.3 %all-reduce.2.cloned.1.call-done = bf16[512,1024]{1,0:T(8,128)(2,1)} async-done(((bf16[512,1024]{1,0:T(8,128)(2,1)}), bf16[512,1024]{1,0:T(8,128)(2,1)}) %all-reduce.2.cloned.1.call-update) | async-done | bytes 1048592 | tf_op jit(solution)/shard_map/psum | solution.py:63
  297.1 0.0 copy-start
  297.1 1.6 convolution_convert_fusion
  298.8 0.1 reshape.69
  298.9 1.0 pad_maximum_fusion
  299.9 13.4 %all-to-all-start.1 = ((bf16[64,2,1025]{2,1,0:T(2,128)(2,1)}), bf16[64,2,1025]{2,1,0:T(2,128)(2,1)S(1)}, u32[]{:S(2)}, u32[]{:S(2)}) async-start(bf16[64,2,1025]{2,1,0:T(2,128)(2,1)} %pad_maximum_fusion), calls=%async_computation.1 | async-start | bytes 589824 | tf_op jit(solution)/shard_map/all_to_all | solution.py:41
  313.3 0.0 copy-done.1
  313.3 0.3 multiply_reduce_fusion.2
  313.6 0.0 copy-done
  313.6 0.3 multiply_reduce_fusion.3
  313.9 1.7 fusion.10
  315.6 10.7 %all-to-all-done.1 = bf16[64,2,1025]{2,1,0:T(2,128)(2,1)S(1)} async-done(((bf16[64,2,1025]{2,1,0:T(2,128)(2,1)}), bf16[64,2,1025]{2,1,0:T(2,128)(2,1)S(1)}, u32[]{:S(2)}, u32[]{:S(2)}) %all-to-all-start.1) | async-done | bytes 262432 | tf_op jit(solution)/shard_map/all_to_all | solution.py:41
  326.3 0.1 convert_reduce_fusion.1
  326.4 0.1 reshape.71
  326.6 0.1 convert_reduce_fusion.2
  326.7 0.2 split.19
  326.9 0.1 reshape.70
  327.0 0.8 convolution_divide_fusion
  (7 shorter events, 0.1 us)
Async XLA Ops:
  7.2 145.3 %all-gather.2.cloned.1.call-start = ((), (), s32[]{:S(2)}) async-start(), calls=%async_computation.2 | async-start | bytes 4792320 | tf_op jit(solution)/shard_map/all_gather | solution.py:32
  10.8 39.1 %all-to-all-start = ((bf16[8,64,1280]{2,1,0:T(8,128)(2,1)}), bf16[8,64,1280]{2,1,0:T(8,128)(2,1)S(1)}, u32[]{:S(2)}, u32[]{:S(2)}) async-start(bf16[8,64,1280]{2,1,0:T(8,128)(2,1)} %broadcast_in_dim.11), calls=%async_computation | async-start | bytes 2621440 | tf_op jit(solution)/shard_map/all_to_all | solution.py:20
  24.1 273.0 %all-reduce.2.cloned.1.call-start = ((), (), s32[]{:S(2)}) async-start(), calls=%async_computation.3 | async-start | bytes 2097152 | tf_op jit(solution)/shard_map/psum | solution.py:63
  154.8 6.3 %copy-start.2 = (s32[512]{0:T(512)S(1)}, s32[512]{0:T(512)}, u32[]{:S(2)}) copy-start(s32[512]{0:T(512)} %param.9) | copy-start | bytes 6148
  161.1 152.2 %copy-start.1 = (bf16[512,1024]{1,0:T(8,128)(2,1)S(1)}, bf16[512,1024]{1,0:T(8,128)(2,1)}, u32[]{:S(2)}) copy-start(bf16[512,1024]{1,0:T(8,128)(2,1)} %param.8) | copy-start | bytes 3145732
  297.1 16.5 %copy-start = (bf16[512,1024]{1,0:T(8,128)(2,1)S(1)}, bf16[512,1024]{1,0:T(8,128)(2,1)}, u32[]{:S(2)}) copy-start(bf16[512,1024]{1,0:T(8,128)(2,1)} %all-reduce.2.cloned.1.call-done) | copy-start | bytes 3145732
  299.9 26.4 %all-to-all-start.1 = ((bf16[64,2,1025]{2,1,0:T(2,128)(2,1)}), bf16[64,2,1025]{2,1,0:T(2,128)(2,1)S(1)}, u32[]{:S(2)}, u32[]{:S(2)}) async-start(bf16[64,2,1025]{2,1,0:T(2,128)(2,1)} %pad_maximum_fusion), calls=%async_computation.1 | async-start | bytes 589824 | tf_op jit(solution)/shard_map/all_to_all | solution.py:41
Sparse Core Ops, SparseCore 0:
  10.7 141.7 all-gather.1
  161.3 135.8 all-reduce.1
where the time goes:
time: 335 us
  waiting for transfers between devices  274 us (82%)
  starting transfers between devices  26.8 us (8%)
  between operations  14.2 us (4%)
  matrix products  10.4 us (3%)
  other arithmetic  6.39 us (2%)
    psum x1, waiting for transfers between devices, local(): features = lax.psum(partial_value.astype(jnp.bfloat16), 'land')  135 us
    all_gather x1, waiting for transfers between devices, sent_together(): whole = lax.all_gather(both, axis, axis=dim, tiled=True)  102 us
    all_to_all x1, waiting for transfers between devices, copy_for_each(): lax.all_to_all(jnp.broadcast_to(shard[None], (devices, *shard.shape)), ax...  25.7 us
    all_to_all x1, starting transfers between devices, in_one_piece(): lax.all_to_all(both, axis, split_axis=split_dim, concat_axis=concat_dim,...  13.4 us
    all_to_all x1, starting transfers between devices, copy_for_each(): lax.all_to_all(jnp.broadcast_to(shard[None], (devices, *shard.shape)), ax...  13.3 us
    all_to_all x1, waiting for transfers between devices, in_one_piece(): lax.all_to_all(both, axis, split_axis=split_dim, concat_axis=concat_dim,...  10.7 us
  transfers between devices with their start and end apart: 4, of which 4 were waited for; matrix products, arithmetic and copies ran while one was open for 2% of the time, Pallas kernels for 0%

commit v1 on v0

v1 whole, which is shorter than its diff:
```python
import functools

import jax
import jax.numpy as jnp
from jax import lax
from jax.experimental import pallas as pl
from jax.experimental.pallas import tpu as pltpu
from jax.sharding import PartitionSpec as P

EPSILON = 1e-06
SHARPNESS = 6.0
MESH = pl.DeviceIdType.MESH
BF16 = jnp.bfloat16
F32 = jnp.float32

NX, NZ, NY = 4, 8, 8
EW = 1280
FW = 1024
Q = 4
QW = FW // Q
H = 2
HW = FW // H
N_SEM = 170

POS = {4: 0, 5: 1, 3: 2, 6: 3, 2: 4, 7: 5, 1: 6, 0: 7}


def kernel(
    e_ref, l_ref, f_ref, c_ref, a_ref,
    dist_ref, newc_ref,
    ebuf, lbuf, fbuf, kbuf, pbuf, rbuf, feat, abuf, obuf, arr, tsend, trecv, csend, crecv,
    rowc, markc, ss, rs,
):
    land = lax.axis_index("land")
    dp = lax.axis_index("dp")
    x, zh = land // 2, land % 2
    zl, y, c = dp // 16, (dp // 2) % 8, dp % 2
    z = zh * 4 + zl

    def device(dx=0, dz=0, dy=0, dc=0):
        xx, zz, yy, cc = (x + dx) % NX, (z + dz) % NZ, (y + dy) % NY, (c + dc) % 2
        return (xx * 2 + zz // 4, (zz % 4) * 16 + yy * 2 + cc)

    def near(rz, rc):
        return (land, ((zl + rz) % 4) * 16 + y * 2 + (c + rc) % 2)

    y_up, y_down = device(dy=1), device(dy=7)
    x_up, x_down = device(dx=1), device(dx=3)
    z_up, z_down = device(dz=1), device(dz=7)
    z_far = device(dz=4)
    sibling = device(dc=1)
    y_peer = {d: device(dy=d) for d in range(1, 8)}
    x_peer = {d: device(dx=d) for d in range(1, 4)}
    zc_peer = {i: near(i // 2, i % 2) for i in range(1, 8)}

    barrier = pltpu.get_barrier_semaphore()
    peers = [*y_peer.values(), *x_peer.values(), z_up, z_down, z_far, *zc_peer.values()]
    for peer in peers:
        pl.semaphore_signal(barrier, inc=1, device_id=peer, device_id_type=MESH)
    pl.semaphore_wait(barrier, len(peers))

    copies = []

    def send(src, dst, peer):
        k = len(copies)
        copy = pltpu.make_async_remote_copy(
            src_ref=src, dst_ref=dst, send_sem=ss.at[k], recv_sem=rs.at[k],
            device_id=peer, device_id_type=MESH,
        )
        copy.start()
        copies.append(copy)
        return copy

    def got(*arrived):
        for copy in arrived:
            copy.wait_recv()

    def send_e(k):
        up = e_ref if k == 1 else ebuf.at[POS[k - 1]]
        down = e_ref if k == 1 else ebuf.at[POS[9 - k]]
        if k < 4:
            return (
                send(up, ebuf.at[POS[k]], y_up),
                send(down, ebuf.at[POS[8 - k]], y_down),
            )
        return (
            send(up.at[pl.ds(0, 32)], ebuf.at[POS[4], pl.ds(0, 32)], y_up),
            send(down.at[pl.ds(32, 32)], ebuf.at[POS[4], pl.ds(32, 32)], y_down),
        )

    def send_lz(k):
        up = l_ref if k == 1 else lbuf.at[0, 0, k - 1]
        down = l_ref if k == 1 else lbuf.at[0, 0, 9 - k]
        if k < 4:
            return (
                send(up, lbuf.at[0, 0, k], z_up),
                send(down, lbuf.at[0, 0, 8 - k], z_down),
            )
        first, second = pl.ds(0, EW // 2), pl.ds(EW // 2, EW // 2)
        return (
            send(up.at[:, first], lbuf.at[0, 0, 4, :, first], z_up),
            send(down.at[:, second], lbuf.at[0, 0, 4, :, second], z_down),
        )

    def send_lx(dz):
        src = l_ref if dz == 0 else lbuf.at[0, 0, dz]
        return (
            send(src, lbuf.at[1, 0, dz], x_up),
            send(src, lbuf.at[3, 0, dz], x_down),
        )

    def send_lx2(dz):
        if dz < 4:
            return send(lbuf.at[1, 0, dz], lbuf.at[2, 0, dz], x_up)
        return send(lbuf.at[3, 0, dz], lbuf.at[2, 0, dz], x_down)

    def send_fz(k):
        up, down = fbuf.at[:, 0, k - 1], fbuf.at[:, 0, (9 - k) % 8]
        if k < 4:
            return (
                send(up, fbuf.at[:, 0, k], z_up),
                send(down, fbuf.at[:, 0, 8 - k], z_down),
            )
        first, second = pl.ds(0, 2), pl.ds(2, 2)
        return (
            send(fbuf.at[first, 0, 3], fbuf.at[first, 0, 4], z_up),
            send(fbuf.at[second, 0, 5], fbuf.at[second, 0, 4], z_down),
        )

    def send_fs(k):
        return send(fbuf.at[:, 0, k], fbuf.at[:, 1, k], sibling)

    def send_ls(dx):
        return send(lbuf.at[dx, 0], lbuf.at[dx, 1], sibling)

    fx1 = (send(f_ref, fbuf.at[1, 0, 0], x_up), send(f_ref, fbuf.at[3, 0, 0], x_down))
    lz = {1: send_lz(1)}
    e = {1: send_e(1)}
    lx = {0: send_lx(0)}
    ids_in = [send(a_ref, abuf.at[d], y_peer[d]) for d in range(1, 8)]
    ebuf[POS[0]] = e_ref[...]
    lbuf[0, 0, 0] = l_ref[...]
    fbuf[0, 0, 0] = f_ref[...]
    abuf[0] = a_ref[...]

    def targets(a):
        block = a >> 3
        to = block & 63
        ry = ((to >> 1) - y) & 7
        rz = ((to >> 4) - zl) & 3
        rc = (to - c) & 1
        at = ry * 8 + rz * 2 + rc
        return jnp.where((block >> 6) == land, at, -1), (a & 7).astype(F32)

    def picks(at, base, count):
        shape = (count, at.shape[1])
        here = jnp.broadcast_to(at, shape) == lax.broadcasted_iota(jnp.int32, shape, 0) + base
        row = lax.broadcasted_iota(jnp.int32, shape, 1).astype(F32)
        first = jnp.min(jnp.where(here, row, 1e4), axis=1, keepdims=True)
        last = jnp.max(jnp.where(here, row, -1.0), axis=1, keepdims=True)
        one = jnp.where(here & (row == first), 1.0, 0.0)
        two = jnp.where(here & (row == last) & (last != first), 1.0, 0.0)
        return one, two

    def across(column):
        n = column.shape[0]
        spread = jnp.broadcast_to(column, (n, n))
        eye = lax.broadcasted_iota(jnp.int32, (n, n), 0) == lax.broadcasted_iota(jnp.int32, (n, n), 1)
        return jnp.sum(jnp.where(eye, spread, 0.0), axis=0, keepdims=True)

    at, _ = targets(a_ref[...])
    one, two = picks(at, 0, 64)
    pick = jnp.concatenate([one.reshape(8, 8, 512), two.reshape(8, 8, 512)], axis=1)
    pick = pick.reshape(128, 512).astype(BF16)

    got(*fx1)
    half_a, half_b = pl.ds(0, FW // 2), pl.ds(FW // 2, FW // 2)
    fx2 = (
        send(fbuf.at[1, 0, 0, :, half_a], fbuf.at[2, 0, 0, :, half_a], x_up),
        send(fbuf.at[3, 0, 0, :, half_b], fbuf.at[2, 0, 0, :, half_b], x_down),
    )
    got(*lz[1])
    lz[2] = send_lz(2)
    lx[1], lx[7] = send_lx(1), send_lx(7)
    got(*fx2)
    fz = {1: send_fz(1)}
    fs = {0: send_fs(0)}
    got(*lz[2])
    lz[3] = send_lz(3)
    lx[2], lx[6] = send_lx(2), send_lx(6)
    got(*e[1])
    e[2] = send_e(2)

    got(*ids_in)
    ids = []
    for d in range(8):
        at, local_id = targets(abuf[d])
        near_at = jnp.where((at >= 0) & ((((abuf[d] >> 4) & 7) - y) & 7 == 0), at & 7, -1)
        for chosen in picks(near_at, 0, 8):
            ids.append(jnp.sum(chosen * (local_id + 1.0), axis=1, keepdims=True) - 1.0)
    ids = across(jnp.concatenate(ids, axis=0))
    row = lax.broadcasted_iota(jnp.int32, (64, 128), 0)
    column = lax.broadcasted_iota(jnp.int32, (64, 128), 1)
    match = ((row >> 3) == (column & 7)) & ((row & 7).astype(F32) == jnp.broadcast_to(ids, (64, 128)))
    match = jnp.where(match, 1.0, 0.0)
    csend[...] = jnp.broadcast_to(jnp.sum(match, axis=1, keepdims=True), (64, 128)).reshape(8, 8, 128)
    match = match.astype(BF16)
    counts_in = [send(csend.at[i], crecv.at[i], zc_peer[i]) for i in range(1, 8)]

    lx2 = {}
    got(*lx[0])
    lx2[0] = send_lx2(0)
    got(*fz[1])
    fz[2] = send_fz(2)
    fs[1], fs[7] = send_fs(1), send_fs(7)
    got(*lz[3])
    lz[4] = send_lz(4)
    lx[3], lx[5] = send_lx(3), send_lx(5)
    got(*lx[1], *lx[7])
    lx2[1], lx2[7] = send_lx2(1), send_lx2(7)
    got(*e[2])
    e[3] = send_e(3)
    got(*fz[2])
    fz[3] = send_fz(3)
    fs[2], fs[6] = send_fs(2), send_fs(6)
    got(*lz[4])
    lx[4] = send_lx(4)
    ls = {0: send_ls(0)}
    got(*lx[2], *lx[6])
    lx2[2], lx2[6] = send_lx2(2), send_lx2(6)

    cents = c_ref[...]
    cent_sq = jnp.sum(jnp.square(cents.astype(F32)), axis=1, keepdims=True)
    cent_sq = jnp.concatenate([across(cent_sq[k * 128 : (k + 1) * 128]) for k in range(4)], axis=1)

    got(*fz[3])
    fz[4] = send_fz(4)
    fs[3], fs[5] = send_fs(3), send_fs(5)
    got(*lx[3], *lx[5], *lx[4])
    lx2[3], lx2[5], lx2[4] = send_lx2(3), send_lx2(5), send_lx2(4)
    ls[1], ls[3] = send_ls(1), send_ls(3)
    got(*e[3])
    e[4] = send_e(4)

    def row_coef(g):
        rows = ebuf[2 * g : 2 * g + 2].reshape(128, EW).astype(F32)
        mean = jnp.sum(rows * rows, axis=1, keepdims=True) * (1.0 / EW)
        rowc[g * 128 : (g + 1) * 128, :] = lax.rsqrt(mean + EPSILON) * (SHARPNESS / EW)

    def mark_coef(dx):
        marks = lbuf[dx].reshape(256, EW).astype(F32)
        mean = jnp.sum(marks * marks, axis=1, keepdims=True) * (1.0 / EW)
        scale = lax.rsqrt(mean + EPSILON)
        markc[dx] = jnp.concatenate([across(scale[:128]), across(scale[128:])], axis=1)

    def similar(g, dx):
        dots = lax.dot_general(
            ebuf[2 * g : 2 * g + 2].reshape(128, EW), lbuf[dx].reshape(256, EW),
            (((1,), (1,)), ((), ())), preferred_element_type=F32,
        )
        rows = slice(g * 128, (g + 1) * 128)
        value = jnp.exp(dots * rowc[rows, :] * markc[dx] - SHARPNESS)
        kbuf[rows, dx * 256 : (dx + 1) * 256] = value.astype(BF16)

    row_coef(3)
    row_coef(2)
    row_coef(1)
    got(ls[0])
    mark_coef(0)
    for g in (3, 2, 1):
        similar(g, 0)
    got(*fz[4])
    fs[4] = send_fs(4)
    got(ls[1], ls[3])
    for dx in (1, 3):
        mark_coef(dx)
        for g in (3, 2, 1):
            similar(g, dx)
    got(*lx2.values())
    ls[2] = send_ls(2)
    got(*e[4])
    row_coef(0)
    for dx in (0, 1, 3):
        similar(0, dx)
    got(ls[2])
    mark_coef(2)
    for g in range(4):
        similar(g, 2)
    got(*fs.values())

    def partial(g):
        for q in range(Q):
            cols = slice(q * QW, (q + 1) * QW)
            value = jnp.dot(
                kbuf[g * 128 : (g + 1) * 128, :], fbuf[:, :, :, :, cols].reshape(1024, QW),
                preferred_element_type=F32,
            )
            pbuf[2 * g : 2 * g + 2, :, cols] = value.reshape(2, 64, QW).astype(BF16)

    def length(q, way):
        return 4 if (q + way) % 2 == 0 else 3

    def slot(q, way, t):
        left = length(q, way) - t
        return POS[left if way == 0 else (8 - left) % 8]

    toward = (y_down, y_up)

    def part(q):
        return pl.ds(q * QW, QW)

    chain = {}

    def begin(q, way):
        chain[q, way] = send(pbuf.at[slot(q, way, 0), :, part(q)], rbuf.at[q, way, 0], toward[way])

    partial(0)
    for q in range(Q):
        begin(q, 0 if q % 2 == 0 else 1)
        if q % 2 == 0:
            begin(q, 1)
    partial(1)
    for q in range(Q):
        if q % 2 == 1:
            begin(q, 0)
    partial(2)
    partial(3)

    def finish(q):
        cols = slice(q * QW, (q + 1) * QW)
        total = pbuf[POS[0], :, cols].astype(F32)
        for way in range(2):
            total += rbuf[q, way, length(q, way) - 1].astype(F32)
        feat[land, :, cols] = total.astype(BF16)
        own = feat.at[land, :, part(q)]
        return send(own, own, z_far), [send(own, own, x_peer[d]) for d in (1, 3, 2)]

    def relay(q):
        other = feat.at[land + 1 - 2 * zh, :, part(q)]
        return [send(other, other, x_peer[d]) for d in (1, 3, 2)]

    gather = {}
    for t in range(1, 5):
        for q in range(Q):
            for way in range(2):
                n = length(q, way)
                if t > n:
                    continue
                got(chain[q, way])
                if t < n:
                    cols = slice(q * QW, (q + 1) * QW)
                    rbuf[q, way, t - 1] = (
                        rbuf[q, way, t - 1].astype(F32) + pbuf[slot(q, way, t), :, cols].astype(F32)
                    ).astype(BF16)
                    chain[q, way] = send(rbuf.at[q, way, t - 1], rbuf.at[q, way, t], toward[way])
            if t == 4:
                gather[q] = finish(q)
    arriving = []
    for q in range(Q):
        far, around = gather[q]
        got(far)
        arriving.append(around + relay(q))

    step1 = {}
    for h in range(H):
        for q in range(h * Q // H, (h + 1) * Q // H):
            got(*arriving[q])
        cols = slice(h * HW, (h + 1) * HW)
        chosen = jnp.dot(pick, feat[:, :, cols].reshape(512, HW), preferred_element_type=F32)
        obuf[:, :, cols] = chosen.reshape(8, 16, HW).astype(BF16)
        arr[0, :, cols] = chosen[:16].astype(BF16)
        ds = pl.ds(h * HW, HW)
        step1[h] = [send(obuf.at[d, :, ds], arr.at[d, :, ds], y_peer[d]) for d in range(1, 8)]

    for b in range(4):
        rows = feat[2 * b : 2 * b + 2].reshape(128, FW)
        wide = rows.astype(F32)
        feat_sq = jnp.sum(wide * wide, axis=1, keepdims=True)
        cross = lax.dot_general(rows, c_ref[...], (((1,), (1,)), ((), ())), preferred_element_type=F32)
        dist_ref[b * 128 : (b + 1) * 128, :] = (feat_sq + cent_sq - 2.0 * cross) * (1.0 / FW)

    step2 = {}
    mine = []
    for h in range(H):
        got(*step1[h])
        cols = slice(h * HW, (h + 1) * HW)
        sums = jnp.dot(match, arr[:, :, cols].reshape(128, HW), preferred_element_type=F32)
        mine.append(sums[:8])
        sums = sums.reshape(8, 8, HW)
        tsend[h] = jnp.concatenate([sums[:, :, : HW // 2], sums[:, :, HW // 2 :]], axis=1).astype(BF16)
        step2[h] = [send(tsend.at[h, i], trecv.at[h, i], zc_peer[i]) for i in range(1, 8)]

    got(*counts_in)
    counts = csend[0]
    for i in range(1, 8):
        counts += crecv[i]
    scale = 1.0 / jnp.maximum(counts[:, :1], 1.0)
    for h in range(H):
        got(*step2[h])
        total = jnp.sum(trecv[h, 1:].astype(F32), axis=0)
        total = mine[h] + jnp.concatenate([total[:8], total[8:]], axis=1)
        newc_ref[:, h * HW : (h + 1) * HW] = total * scale

    for copy in copies:
        copy.wait_send()


def local(embeddings, landmarks, factor, centroids, assignment):
    vmem = pl.BlockSpec(memory_space=pltpu.VMEM)
    return pl.pallas_call(
        kernel,
        out_shape=(
            jax.ShapeDtypeStruct((512, 512), F32),
            jax.ShapeDtypeStruct((8, FW), F32),
        ),
        in_specs=[vmem] * 5,
        out_specs=(vmem, vmem),
        scratch_shapes=[
            pltpu.VMEM((8, 64, EW), BF16),
            pltpu.VMEM((4, 2, 8, 16, EW), BF16),
            pltpu.VMEM((4, 2, 8, 16, FW), BF16),
            pltpu.VMEM((512, 1024), BF16),
            pltpu.VMEM((8, 64, FW), BF16),
            pltpu.VMEM((Q, 2, 4, 64, QW), BF16),
            pltpu.VMEM((8, 64, FW), BF16),
            pltpu.VMEM((8, 1, 512), jnp.int32),
            pltpu.VMEM((8, 16, FW), BF16),
            pltpu.VMEM((8, 16, FW), BF16),
            pltpu.VMEM((H, 8, 16, HW // 2), BF16),
            pltpu.VMEM((H, 8, 16, HW // 2), BF16),
            pltpu.VMEM((8, 8, 128), F32),
            pltpu.VMEM((8, 8, 128), F32),
            pltpu.VMEM((512, 1), F32),
            pltpu.VMEM((4, 1, 256), F32),
            pltpu.SemaphoreType.DMA((N_SEM,)),
            pltpu.SemaphoreType.DMA((N_SEM,)),
        ],
        compiler_params=pltpu.CompilerParams(
            collective_id=0, has_side_effects=True, vmem_limit_bytes=48 << 20
        ),
        name="nystrom",
    )(embeddings, landmarks, factor, centroids, assignment.reshape(1, 512))


def solution(mesh):
    return jax.shard_map(
        local,
        mesh=mesh,
        in_specs=(
            P(("dp", "land"), None),
            P(("land", "dp"), None),
            P(("land", "dp"), None),
            P("land", None),
            P("dp"),
        ),
        out_specs=(P("dp", "land"), P(("land", "dp"), None)),
        check_vma=False,
    )
```

time: 335 us -> 92.3 us (0.28)
  waiting for transfers between devices: 274 us -> 0 us
  Pallas kernels: 0 us -> 85.4 us
  starting transfers between devices: 26.8 us -> 0 us
  between operations: 14.2 us -> 0.65 us
  matrix products: 10.4 us -> 0 us
  other arithmetic: 6.39 us -> 0 us
    psum x1 -> x0, waiting for transfers between devices: 135 us -> none  [local(): features = lax.psum(partial_value.astype(jnp.bfloat16), 'land')]
    all_gather x1 -> x0, waiting for transfers between devices: 102 us -> none  [sent_together(): whole = lax.all_gather(both, axis, axis=dim, tiled=True)]
    pallas_call x0 -> x1, Pallas kernels: none -> 85.4 us  [local(): pl.pallas_call(kernel, out_shape=(jax.ShapeDtypeStruct((512, 512), F32),...]
    all_to_all x2 -> x0, waiting for transfers between devices: 36.4 us -> none  [the longest x1 25.7 us: copy_for_each(): lax.all_to_all(jnp.broadcast_to(shard[None], (devices, *shard.shape)), ax...]
    all_to_all x2 -> x0, starting transfers between devices: 26.7 us -> none  [the longest x1 13.4 us: in_one_piece(): lax.all_to_all(both, axis, split_axis=split_dim, concat_axis=concat_dim,...]
    dot_general x4 -> x0, matrix products: 10.4 us -> none  [the longest x1 6.28 us: local(): jnp.dot(jnp.exp(SHARPNESS * (similarity - 1.0)).astype(jnp.bfloat16), fac...]
    unnamed x6 -> x12, local copies, waits for them, and re-layouts: 0.01 us -> 5.94 us
    reduce_sum x6 -> x0, other arithmetic: 3.6 us -> none  [the longest x1 2.32 us: local(): jnp.mean(jnp.square(mark_rows.astype(jnp.float32)), axis=1) + EPSILON]
  transfers between devices with their start and end apart: 4 -> 0, of which waited for: 4 -> 0; matrix products, arithmetic and copies ran while one was open for 2% -> 0% of each run, Pallas kernels for 0% -> 0%
where the time goes in v1:
time: 92.3 us; the launch traced here: 92 us
  Pallas kernels  85.4 us (93%)
  local copies, waits for them, and re-layouts  5.94 us (6%)
    pallas_call x1, Pallas kernels, local(): pl.pallas_call(kernel, out_shape=(jax.ShapeDtypeStruct((512, 512), F32),...  85.4 us
    unnamed x12, local copies, waits for them, and re-layouts  5.94 us

profile of v1, /device:TPU:1, one launch (start us, length us, event | category | flops | bytes accessed | tf_op | source)
XLA Modules:
  0.0 92.0 jit_solution(3302378341048503695)
XLA Ops:
  0.6 0.0 copy-start
  0.6 1.2 %copy-done = bf16[512,1024]{1,0:T(8,128)(2,1)S(1)} copy-done((bf16[512,1024]{1,0:T(8,128)(2,1)S(1)}, bf16[512,1024]{1,0:T(8,128)(2,1)}, u32[]{:S(2)}) %copy-start) | copy-done | bytes 1048600
  1.9 0.0 copy-start.1
  1.9 0.9 copy-done.1
  2.8 0.0 copy-start.2
  2.8 0.8 copy-done.2
  3.6 0.0 copy-start.3
  3.6 0.8 copy-done.3
  4.3 0.0 copy-start.4
  4.3 0.7 copy-done.4
  5.0 85.4 %nystrom.1 = (f32[512,512]{1,0:T(8,128)S(1)}, f32[8,1024]{1,0:T(8,128)S(1)}) custom-call(bf16[64,1280]{1,0:T(8,128)(2,1)S(1)} %copy-done.1, bf16[16,1280]{1,0:T(8,128)(2,1)S(1)} %copy-done.2, bf16[16,1024]{1,0:T(8,128)(2,1)S(1)} %copy-done.3, bf16[512,1024]{1,0:T(8,128)(2,1)S(1)} %copy-done, s32[1,512]{1,0:T(1,128)S(1)} %bitcast.1), custom_call_target="tpu_custom_call" | custom-call | tf_op jit(solution)/shard_map/nystrom/pallas_call | solution.py:410
  90.4 1.0 %copy.9 = f32[512,512]{1,0:T(8,128)} copy(f32[512,512]{1,0:T(8,128)S(1)} %get-tuple-element.4) | data formatting | bytes 2097152
  91.4 0.6 copy.10
Async XLA Ops:
  0.6 1.2 %copy-start = (bf16[512,1024]{1,0:T(8,128)(2,1)S(1)}, bf16[512,1024]{1,0:T(8,128)(2,1)}, u32[]{:S(2)}) copy-start(bf16[512,1024]{1,0:T(8,128)(2,1)} %c_ref.1) | copy-start | bytes 3145732
  1.9 0.9 copy-start.1
  2.8 0.8 copy-start.2
  3.6 0.8 copy-start.3
  4.3 0.7 copy-start.4

commit v2 on v0

v2 whole, which is shorter than its diff:
```python
import jax
import jax.numpy as jnp
from jax import lax
from jax.experimental import pallas as pl
from jax.experimental.pallas import tpu as pltpu
from jax.sharding import PartitionSpec as P

EPSILON = 1e-06
SHARPNESS = 6.0
MESH = pl.DeviceIdType.MESH
BF16 = jnp.bfloat16
F32 = jnp.float32

NX, NZ, NY = 4, 8, 8
EW = 1280
FW = 1024
Q = 4
QW = FW // Q
H = 2
HW = FW // H
N_SEM = 200

POS = {4: 0, 5: 1, 3: 2, 6: 3, 2: 4, 7: 5, 1: 6, 0: 7}

PER_KB = 0.02
PER_KB_SIBLING = 0.002
HOP = 1.4
STEP = 0.05


class Node:
    def __init__(self, needs, work=None, cost=0.0, rank=0.0, copy=None, links=(), hops=1, kb=0.0):
        self.needs, self.work, self.cost, self.rank = needs, work, cost, rank
        self.copy, self.links, self.hops, self.kb = copy, links, hops, kb


def emit(nodes, flying):
    clock, free, done = 0.0, {}, set()
    flying = [(HOP, k, node) for k, node in enumerate(flying)]
    waiting = list(nodes)
    count = len(flying)
    while waiting or flying:
        ready = [n for n in waiting if all(id(d) in done for d in n.needs)]
        sends = [n for n in ready if n.copy is not None]
        if sends:
            node = min(sends, key=lambda n: n.rank)
            node.copy.start()
            end = clock
            for link, hops in node.links:
                rate = PER_KB_SIBLING if link == "c" else PER_KB
                free[link] = max(clock, free.get(link, 0.0)) + node.kb * rate * hops
                end = max(end, free[link])
            flying.append((end + HOP + 0.4 * (node.hops - 1), count, node))
            count += 1
            clock += STEP
            waiting.remove(node)
            continue
        tasks = [n for n in ready if n.copy is None]
        soonest = min(flying) if flying else None
        if soonest and (soonest[0] <= clock or not tasks):
            flying.remove(soonest)
            (soonest[2].copy.wait_recv if soonest[2].links else soonest[2].copy.wait)()
            clock = max(clock, soonest[0]) + STEP
            done.add(id(soonest[2]))
            continue
        node = min(tasks, key=lambda n: n.rank)
        node.work()
        clock += node.cost
        done.add(id(node))
        waiting.remove(node)


def across(column):
    n = column.shape[0]
    spread = jnp.broadcast_to(column, (n, n))
    eye = lax.broadcasted_iota(jnp.int32, (n, n), 0) == lax.broadcasted_iota(jnp.int32, (n, n), 1)
    return jnp.sum(jnp.where(eye, spread, 0.0), axis=0, keepdims=True)


def kernel(
    e_ref, l_ref, f_ref, c_ref, a_ref,
    dist_ref, newc_ref,
    ebuf, lbuf, fbuf, cbuf, kbuf, pbuf, rbuf, feat, abuf, obuf, arr, tsend, trecv, csend, crecv,
    rowc, markc, centq, pickb, matchb, mine, ss, rs, ls,
):
    land = lax.axis_index("land")
    dp = lax.axis_index("dp")
    x, zh = land // 2, land % 2
    zl, y, c = dp // 16, (dp // 2) % 8, dp % 2
    z = zh * 4 + zl

    def device(dx=0, dz=0, dy=0, dc=0):
        xx, zz, yy, cc = (x + dx) % NX, (z + dz) % NZ, (y + dy) % NY, (c + dc) % 2
        return (xx * 2 + zz // 4, (zz % 4) * 16 + yy * 2 + cc)

    def near(rz, rc):
        return (land, ((zl + rz) % 4) * 16 + y * 2 + (c + rc) % 2)

    y_up, y_down = device(dy=1), device(dy=7)
    x_up, x_down = device(dx=1), device(dx=3)
    z_up, z_down = device(dz=1), device(dz=7)
    z_far = device(dz=4)
    sibling = device(dc=1)
    y_peer = {d: device(dy=d) for d in range(1, 8)}
    x_peer = {d: device(dx=d) for d in range(1, 4)}
    zc_peer = {i: near(i // 2, i % 2) for i in range(1, 8)}

    loads = []
    for src, dst in (
        (l_ref, lbuf.at[0, 0, 0]), (f_ref, fbuf.at[0, 0, 0]), (e_ref, ebuf.at[POS[0]]),
        (a_ref, abuf.at[0]), (c_ref, cbuf),
    ):
        copy = pltpu.make_async_copy(src, dst, ls.at[len(loads)])
        copy.start()
        loads.append(Node([], copy=copy))
    got_l, got_f, got_e, got_a, got_c = loads

    barrier = pltpu.get_barrier_semaphore()
    peers = [*y_peer.values(), *x_peer.values(), z_up, z_down, z_far, *zc_peer.values()]
    for peer in peers:
        pl.semaphore_signal(barrier, inc=1, device_id=peer, device_id_type=MESH)
    pl.semaphore_wait(barrier, len(peers))

    nodes = []
    copies = []

    def task(work, cost, needs, rank=0.0):
        nodes.append(Node(needs, work=work, cost=cost, rank=rank))
        return nodes[-1]

    def send(src, dst, peer, links, kb, needs, hops=1, rank=0.0):
        k = len(copies)
        copies.append(
            pltpu.make_async_remote_copy(
                src_ref=src, dst_ref=dst, send_sem=ss.at[k], recv_sem=rs.at[k],
                device_id=peer, device_id_type=MESH,
            )
        )
        nodes.append(Node(needs, copy=copies[k], links=links, kb=kb, hops=hops, rank=rank))
        return nodes[-1]

    YU, YD, XU, XD, ZU, ZD, SC = [((name, 1),) for name in ("y+", "y-", "x+", "x-", "z+", "z-", "c")]

    def far_y(d):
        return (("y+", d),) if d < 4 else (("y-", 8 - d),) if d > 4 else (("y+", 2), ("y-", 2))

    def far_x(d):
        return {1: XU, 3: XD, 2: (("x+", 1), ("x-", 1))}[d]

    fx = {0: got_f}
    fx[1] = send(fbuf.at[0, 0, 0], fbuf.at[1, 0, 0], x_up, XU, 32, [got_f])
    fx[3] = send(fbuf.at[0, 0, 0], fbuf.at[3, 0, 0], x_down, XD, 32, [got_f])
    half_a, half_b = pl.ds(0, FW // 2), pl.ds(FW // 2, FW // 2)
    fx2 = [
        send(fbuf.at[1, 0, 0, :, half_a], fbuf.at[2, 0, 0, :, half_a], x_up, XU, 16, [fx[1]]),
        send(fbuf.at[3, 0, 0, :, half_b], fbuf.at[2, 0, 0, :, half_b], x_down, XD, 16, [fx[3]]),
    ]

    lz = {0: [got_l]}
    for k in range(1, 4):
        lz[k] = [send(lbuf.at[0, 0, k - 1], lbuf.at[0, 0, k], z_up, ZU, 40, lz[k - 1])]
        lz[8 - k] = [send(lbuf.at[0, 0, (9 - k) % 8], lbuf.at[0, 0, 8 - k], z_down, ZD, 40, lz[(9 - k) % 8])]
    first, second = pl.ds(0, EW // 2), pl.ds(EW // 2, EW // 2)
    lz[4] = [
        send(lbuf.at[0, 0, 3, :, first], lbuf.at[0, 0, 4, :, first], z_up, ZU, 20, lz[3]),
        send(lbuf.at[0, 0, 5, :, second], lbuf.at[0, 0, 4, :, second], z_down, ZD, 20, lz[5]),
    ]

    half = [pl.ds(0, 32), pl.ds(32, 32)]
    e = {(0, 0): [got_e], (0, 1): [got_e]}
    for k in range(1, 5):
        for p in range(2):
            up, down = (k - 1, p), ((9 - k) % 8, p)
            if k < 4 or p == 0:
                e[k, p] = [send(ebuf.at[POS[up[0]], half[p]], ebuf.at[POS[k], half[p]], y_up, YU, 80, e[up])]
            if k < 4 or p == 1:
                e[8 - k, p] = [send(ebuf.at[POS[down[0]], half[p]], ebuf.at[POS[8 - k], half[p]], y_down, YD, 80, e[down])]

    lx = {}
    for dz in (0, 1, 7, 2, 6, 3, 5, 4):
        lx[0, dz] = lz[dz]
        lx[1, dz] = [send(lbuf.at[0, 0, dz], lbuf.at[1, 0, dz], x_up, XU, 40, lz[dz])]
        lx[3, dz] = [send(lbuf.at[0, 0, dz], lbuf.at[3, 0, dz], x_down, XD, 40, lz[dz])]
    for dz in (0, 1, 7, 2, 6, 3, 5, 4):
        if dz < 4:
            lx[2, dz] = [send(lbuf.at[1, 0, dz], lbuf.at[2, 0, dz], x_up, XU, 40, lx[1, dz])]
        else:
            lx[2, dz] = [send(lbuf.at[3, 0, dz], lbuf.at[2, 0, dz], x_down, XD, 40, lx[3, dz])]

    fz = {(0, 0): [got_f], (1, 0): [fx[1]], (3, 0): [fx[3]], (2, 0): fx2}
    for k in range(1, 4):
        for dx in (0, 1, 3, 2):
            up, down = (dx, k - 1), (dx, (9 - k) % 8)
            fz[dx, k] = [send(fbuf.at[dx, 0, up[1]], fbuf.at[dx, 0, k], z_up, ZU, 32, fz[up], rank=0.1)]
            fz[dx, 8 - k] = [send(fbuf.at[dx, 0, down[1]], fbuf.at[dx, 0, 8 - k], z_down, ZD, 32, fz[down], rank=0.1)]
    for dx in (0, 1):
        fz[dx, 4] = [send(fbuf.at[dx, 0, 3], fbuf.at[dx, 0, 4], z_up, ZU, 32, fz[dx, 3], rank=0.1)]
    for dx in (3, 2):
        fz[dx, 4] = [send(fbuf.at[dx, 0, 5], fbuf.at[dx, 0, 4], z_down, ZD, 32, fz[dx, 5], rank=0.1)]

    lsib = {}
    for dx in range(4):
        lsib[dx] = [
            send(
                lbuf.at[dx, 0, pl.ds(4 * p, 4)], lbuf.at[dx, 1, pl.ds(4 * p, 4)], sibling, SC, 160,
                [n for dz in range(4 * p, 4 * p + 4) for n in lx[dx, dz]],
            )
            for p in range(2)
        ]
    fsib = [
        send(fbuf.at[:, 0, k], fbuf.at[:, 1, k], sibling, SC, 128, [n for dx in range(4) for n in fz[dx, k]])
        for k in range(8)
    ]

    def targets(a):
        to = (a >> 3) & 63
        ry, rz, rc = ((to >> 1) - y) & 7, ((to >> 4) - zl) & 3, (to - c) & 1
        return (a >> 9) == land, ry, rz * 2 + rc

    def picks(at, at_row):
        row = lax.broadcasted_iota(jnp.int32, at.shape, 1).astype(F32)
        here = at == at_row
        first = jnp.min(jnp.where(here, row, 1e4), axis=1, keepdims=True)
        last = jnp.max(jnp.where(here, row, -1.0), axis=1, keepdims=True)
        one = jnp.where(here & (row == first), 1.0, 0.0)
        two = jnp.where(here & (row == last) & (last != first), 1.0, 0.0)
        return one, two

    def choose():
        inside, ry, rzc = targets(abuf[0])
        at = jnp.broadcast_to(jnp.where(inside, ry * 8 + rzc, -1), (64, 512))
        one, two = picks(at, lax.broadcasted_iota(jnp.int32, (64, 512), 0))
        both = jnp.concatenate([one.reshape(8, 8, 512), two.reshape(8, 8, 512)], axis=1)
        pickb[...] = both.reshape(128, 512).astype(BF16)

    chosen = task(choose, 1.0, [got_a], rank=1.0)

    ids_in = [send(abuf.at[0], abuf.at[d], y_peer[d], far_y(d), 2, [got_a], rank=0.05) for d in range(1, 8)]

    def matching():
        a = abuf[...]
        inside, ry, rzc = targets(a)
        at = jnp.broadcast_to(jnp.where(inside & (ry == 0), rzc, -1), (8, 8, 512)).reshape(64, 512)
        number = jnp.broadcast_to((a & 7).astype(F32) + 1.0, (8, 8, 512)).reshape(64, 512)
        ids = [
            jnp.sum(which * number, axis=1, keepdims=True).reshape(8, 8, 1)
            for which in picks(at, lax.broadcasted_iota(jnp.int32, (64, 512), 0) & 7)
        ]
        ids = across(jnp.concatenate(ids, axis=1).reshape(128, 1)) - 1.0
        row = lax.broadcasted_iota(jnp.int32, (64, 128), 0)
        column = lax.broadcasted_iota(jnp.int32, (64, 128), 1)
        match = ((row >> 3) == (column & 7)) & ((row & 7).astype(F32) == jnp.broadcast_to(ids, (64, 128)))
        match = jnp.where(match, 1.0, 0.0)
        csend[...] = jnp.broadcast_to(jnp.sum(match, axis=1, keepdims=True), (64, 128)).reshape(8, 8, 128)
        matchb[...] = match.astype(BF16)

    matched = task(matching, 1.2, [got_a, *ids_in], rank=8.0)
    counts_in = [send(csend.at[i], crecv.at[i], zc_peer[i], SC, 4, [matched], rank=0.2) for i in range(1, 8)]

    def square_centroids(k):
        def work():
            rows = cbuf[k * 128 : (k + 1) * 128, :].astype(F32)
            centq[:, k * 128 : (k + 1) * 128] = across(jnp.sum(rows * rows, axis=1, keepdims=True))
        return task(work, 0.4, [got_c], rank=9.0)

    squared = [square_centroids(k) for k in range(4)]

    places = {pos: j for j, pos in POS.items()}

    def e_group(g):
        return [n for j in (places[2 * g], places[2 * g + 1]) for p in range(2) for n in e[j, p]]

    def l_group(dx):
        return lsib[dx] + [n for dz in range(8) for n in lx[dx, dz]]

    def row_coef(g):
        def work():
            rows = ebuf[2 * g : 2 * g + 2].reshape(128, EW).astype(F32)
            mean = jnp.sum(rows * rows, axis=1, keepdims=True) * (1.0 / EW)
            rowc[g * 128 : (g + 1) * 128, :] = lax.rsqrt(mean + EPSILON) * (SHARPNESS / EW)
        return task(work, 0.3, e_group(g), rank=2.0)

    def mark_coef(dx):
        def work():
            marks = lbuf[dx].reshape(256, EW).astype(F32)
            mean = jnp.sum(marks * marks, axis=1, keepdims=True) * (1.0 / EW)
            scale = lax.rsqrt(mean + EPSILON)
            markc[dx] = jnp.concatenate([across(scale[:128]), across(scale[128:])], axis=1)
        return task(work, 0.5, l_group(dx), rank=2.0)

    row_done = [row_coef(g) for g in range(4)]
    mark_done = [mark_coef(dx) for dx in range(4)]

    def similar(g, dx):
        def work():
            dots = lax.dot_general(
                ebuf[2 * g : 2 * g + 2].reshape(128, EW), lbuf[dx].reshape(256, EW),
                (((1,), (1,)), ((), ())), preferred_element_type=F32,
            )
            rows = slice(g * 128, (g + 1) * 128)
            value = jnp.exp(dots * rowc[rows, :] * markc[dx] - SHARPNESS)
            kbuf[rows, dx * 256 : (dx + 1) * 256] = value.astype(BF16)
        return task(work, 0.35, [row_done[g], mark_done[dx]], rank=3.0 + 0.1 * g)

    tiles = {(g, dx): similar(g, dx) for g in range(4) for dx in range(4)}

    factor_in = [*fsib, *(n for pieces in fz.values() for n in pieces)]

    def partial(g, q):
        def work():
            cols = slice(q * QW, (q + 1) * QW)
            value = jnp.dot(
                kbuf[g * 128 : (g + 1) * 128, :], fbuf[:, :, :, :, cols].reshape(1024, QW),
                preferred_element_type=F32,
            )
            pbuf[2 * g : 2 * g + 2, :, cols] = value.reshape(2, 64, QW).astype(BF16)
        return task(work, 0.25, [*factor_in, *(tiles[g, dx] for dx in range(4))], rank=4.0 + g)

    parts = {(g, q): partial(g, q) for g in range(4) for q in range(Q)}

    def part(q):
        return pl.ds(q * QW, QW)

    def chain(q, way):
        steps = 4 if (q + way) % 2 == 0 else 3
        peer, link = ((y_down, YD), (y_up, YU))[way]
        slots = [POS[(left if way == 0 else 8 - left) % 8] for left in range(steps, 0, -1)]
        src, needs = pbuf.at[slots[0], :, part(q)], [parts[slots[0] // 2, q]]
        for t in range(steps):
            arrived = send(src, rbuf.at[q, way, t], peer, link, 32, needs, rank=0.01 * q)
            if t < steps - 1:
                def add(t=t, pos=slots[t + 1]):
                    rbuf[q, way, t] = (
                        rbuf[q, way, t].astype(F32) + pbuf[pos, :, q * QW : (q + 1) * QW].astype(F32)
                    ).astype(BF16)
                needs = [task(add, 0.06, [arrived, parts[slots[t + 1] // 2, q]], rank=0.0)]
                src = rbuf.at[q, way, t]
        return arrived, steps - 1

    chunk_in = []
    for q in range(Q):
        ends = [chain(q, way) for way in range(2)]

        def finish(q=q, ends=ends):
            cols = slice(q * QW, (q + 1) * QW)
            total = pbuf[POS[0], :, cols].astype(F32)
            for way in range(2):
                total += rbuf[q, way, ends[way][1]].astype(F32)
            feat[land, :, cols] = total.astype(BF16)

        finished = task(finish, 0.1, [parts[POS[0] // 2, q], *(arrived for arrived, _ in ends)], rank=0.0)
        own = feat.at[land, :, part(q)]
        far = send(own, own, z_far, (("z+", 2), ("z-", 2)), 32, [finished], hops=4)
        other = feat.at[land + 1 - 2 * zh, :, part(q)]
        chunk_in.append([finished, far])
        for piece, need in ((own, finished), (other, far)):
            chunk_in[q] += [
                send(piece, piece, x_peer[d], far_x(d), 32, [need], hops=1 + d % 2) for d in (2, 1, 3)
            ]

    step2 = []
    summed = []
    for h in range(H):
        cols = slice(h * HW, (h + 1) * HW)
        ds = pl.ds(h * HW, HW)

        def select(cols=cols):
            out = jnp.dot(pickb[...], feat[:, :, cols].reshape(512, HW), preferred_element_type=F32)
            obuf[:, :, cols] = out.reshape(8, 16, HW).astype(BF16)
            arr[0, :, cols] = out[:16].astype(BF16)

        chunks = [n for q in range(h * Q // H, (h + 1) * Q // H) for n in chunk_in[q]]
        selected = task(select, 0.3, [chosen, *chunks], rank=0.5)
        step1 = [
            send(obuf.at[d, :, ds], arr.at[d, :, ds], y_peer[d], far_y(d), 16, [selected], hops=min(d, 8 - d))
            for d in (4, 3, 5, 2, 6, 1, 7)
        ]

        def sum_up(h=h, cols=cols):
            sums = jnp.dot(matchb[...], arr[:, :, cols].reshape(128, HW), preferred_element_type=F32)
            mine[:, cols] = sums[:8]
            sums = sums.reshape(8, 8, HW)
            tsend[h] = jnp.concatenate([sums[:, :, : HW // 2], sums[:, :, HW // 2 :]], axis=1).astype(BF16)

        summed.append(task(sum_up, 0.3, [matched, selected, *step1], rank=0.6))
        step2 += [
            send(
                tsend.at[h, i], trecv.at[h, i], zc_peer[i],
                SC if i == 1 else ((("z+", 1), ("z-", 1))), 8, [summed[h]], hops=2,
            )
            for i in (7, 6, 5, 4, 3, 2, 1)
        ]

    def distances(b):
        def work():
            rows = feat[2 * b : 2 * b + 2].reshape(128, FW)
            wide = rows.astype(F32)
            feat_sq = jnp.sum(wide * wide, axis=1, keepdims=True)
            cross = lax.dot_general(rows, cbuf[...], (((1,), (1,)), ((), ())), preferred_element_type=F32)
            dist_ref[b * 128 : (b + 1) * 128, :] = (feat_sq + centq[...] - 2.0 * cross) * (1.0 / FW)
        return task(work, 0.5, [got_c, *squared, *(n for chunk in chunk_in for n in chunk)], rank=10.0)

    for b in range(4):
        distances(b)

    def means():
        counts = csend[0]
        for i in range(1, 8):
            counts += crecv[i]
        scale = 1.0 / jnp.maximum(counts[:, :1], 1.0)
        for h in range(H):
            total = jnp.sum(trecv[h, 1:].astype(F32), axis=0)
            total = mine[:, h * HW : (h + 1) * HW] + jnp.concatenate([total[:8], total[8:]], axis=1)
            newc_ref[:, h * HW : (h + 1) * HW] = total * scale

    task(means, 0.2, [*summed, *step2, *counts_in], rank=0.7)

    emit(nodes, loads)
    for copy in copies:
        copy.wait_send()


def local(embeddings, landmarks, factor, centroids, assignment):
    vmem = pl.BlockSpec(memory_space=pltpu.VMEM)
    anywhere = pl.BlockSpec(memory_space=pl.ANY)
    return pl.pallas_call(
        kernel,
        out_shape=(
            jax.ShapeDtypeStruct((512, 512), F32),
            jax.ShapeDtypeStruct((8, FW), F32),
        ),
        in_specs=[anywhere] * 5,
        out_specs=(vmem, vmem),
        scratch_shapes=[
            pltpu.VMEM((8, 64, EW), BF16),
            pltpu.VMEM((4, 2, 8, 16, EW), BF16),
            pltpu.VMEM((4, 2, 8, 16, FW), BF16),
            pltpu.VMEM((512, FW), BF16),
            pltpu.VMEM((512, 1024), BF16),
            pltpu.VMEM((8, 64, FW), BF16),
            pltpu.VMEM((Q, 2, 4, 64, QW), BF16),
            pltpu.VMEM((8, 64, FW), BF16),
            pltpu.VMEM((8, 1, 512), jnp.int32),
            pltpu.VMEM((8, 16, FW), BF16),
            pltpu.VMEM((8, 16, FW), BF16),
            pltpu.VMEM((H, 8, 16, HW // 2), BF16),
            pltpu.VMEM((H, 8, 16, HW // 2), BF16),
            pltpu.VMEM((8, 8, 128), F32),
            pltpu.VMEM((8, 8, 128), F32),
            pltpu.VMEM((512, 1), F32),
            pltpu.VMEM((4, 1, 256), F32),
            pltpu.VMEM((1, 512), F32),
            pltpu.VMEM((128, 512), BF16),
            pltpu.VMEM((64, 128), BF16),
            pltpu.VMEM((8, FW), F32),
            pltpu.SemaphoreType.DMA((N_SEM,)),
            pltpu.SemaphoreType.DMA((N_SEM,)),
            pltpu.SemaphoreType.DMA((5,)),
        ],
        compiler_params=pltpu.CompilerParams(
            collective_id=0, has_side_effects=True, vmem_limit_bytes=56 << 20
        ),
        name="nystrom",
    )(embeddings, landmarks, factor, centroids, assignment.reshape(1, 512))


def solution(mesh):
    return jax.shard_map(
        local,
        mesh=mesh,
        in_specs=(
            P(("dp", "land"), None),
            P(("land", "dp"), None),
            P(("land", "dp"), None),
            P("land", None),
            P("dp"),
        ),
        out_specs=(P("dp", "land"), P(("land", "dp"), None)),
        check_vma=False,
    )
```

time: 335 us -> 89 us (0.27)
  waiting for transfers between devices: 274 us -> 0 us
  Pallas kernels: 0 us -> 85.3 us
  starting transfers between devices: 26.8 us -> 0 us
  between operations: 14.2 us -> 0.65 us
  matrix products: 10.4 us -> 0 us
  other arithmetic: 6.39 us -> 0 us
    psum x1 -> x0, waiting for transfers between devices: 135 us -> none  [local(): features = lax.psum(partial_value.astype(jnp.bfloat16), 'land')]
    all_gather x1 -> x0, waiting for transfers between devices: 102 us -> none  [sent_together(): whole = lax.all_gather(both, axis, axis=dim, tiled=True)]
    pallas_call x0 -> x1, Pallas kernels: none -> 85.3 us  [local(): pl.pallas_call(kernel, out_shape=(jax.ShapeDtypeStruct((512, 512), F32),...]
    all_to_all x2 -> x0, waiting for transfers between devices: 36.4 us -> none  [the longest x1 25.7 us: copy_for_each(): lax.all_to_all(jnp.broadcast_to(shard[None], (devices, *shard.shape)), ax...]
    all_to_all x2 -> x0, starting transfers between devices: 26.7 us -> none  [the longest x1 13.4 us: in_one_piece(): lax.all_to_all(both, axis, split_axis=split_dim, concat_axis=concat_dim,...]
    dot_general x4 -> x0, matrix products: 10.4 us -> none  [the longest x1 6.28 us: local(): jnp.dot(jnp.exp(SHARPNESS * (similarity - 1.0)).astype(jnp.bfloat16), fac...]
    reduce_sum x6 -> x0, other arithmetic: 3.6 us -> none  [the longest x1 2.32 us: local(): jnp.mean(jnp.square(mark_rows.astype(jnp.float32)), axis=1) + EPSILON]
  transfers between devices with their start and end apart: 4 -> 0, of which waited for: 4 -> 0; matrix products, arithmetic and copies ran while one was open for 2% -> 0% of each run, Pallas kernels for 0% -> 0%
where the time goes in v2:
time: 89 us; the launch traced here: 88.9 us
  Pallas kernels  85.3 us (96%)
  local copies, waits for them, and re-layouts  2.89 us (3%)
    pallas_call x1, Pallas kernels, local(): pl.pallas_call(kernel, out_shape=(jax.ShapeDtypeStruct((512, 512), F32),...  85.3 us
    unnamed x4, local copies, waits for them, and re-layouts  2.89 us

profile of v2, /device:TPU:1, one launch (start us, length us, event | category | flops | bytes accessed | tf_op | source)
XLA Modules:
  0.0 88.9 jit_solution(2455389324857546085)
XLA Ops:
  0.6 85.3 %nystrom.1 = (f32[512,512]{1,0:T(8,128)}, f32[8,1024]{1,0:T(8,128)}) custom-call(bf16[64,1280]{1,0:T(8,128)(2,1)} %e_ref.1, bf16[16,1280]{1,0:T(8,128)(2,1)} %l_ref.1, bf16[16,1024]{1,0:T(8,128)(2,1)} %f_ref.1, bf16[512,1024]{1,0:T(8,128)(2,1)} %c_ref.1, s32[1,512]{1,0:T(1,128)} %bitcast.1), custom_call_target="tpu_custom_call" | custom-call | tf_op jit(solution)/shard_map/nystrom/pallas_call | solution.py:426
  86.0 0.0 copy-start
  86.0 2.3 %copy.9 = f32[512,512]{1,0:T(8,128)} copy(f32[512,512]{1,0:T(8,128)} %get-tuple-element.4) | data formatting | bytes 2097152
  88.2 0.0 copy-done
  88.2 0.6 copy.10
Async XLA Ops:
  86.0 2.3 %copy-start = (f32[8,1024]{1,0:T(8,128)S(1)}, f32[8,1024]{1,0:T(8,128)}, u32[]{:S(2)}) copy-start(f32[8,1024]{1,0:T(8,128)} %get-tuple-element.5) | copy-start | bytes 98308

commit v3 on v2

--- a/solution.py
+++ b/solution.py
@@ -18,14 +18,18 @@
 QW = FW // Q
 H = 2
 HW = FW // H
-N_SEM = 200
+N_SEM = 330
 
 POS = {4: 0, 5: 1, 3: 2, 6: 3, 2: 4, 7: 5, 1: 6, 0: 7}
 
 PER_KB = 0.02
 PER_KB_SIBLING = 0.002
-HOP = 1.4
-STEP = 0.05
+HOP = 3.6
+FURTHER = 0.95
+EP = 4
+FH = 2
+LXU = (4,)
+STEP = 0.025
 
 
 class Node:
@@ -35,8 +39,8 @@
 
 
 def emit(nodes, flying):
-    clock, free, done = 0.0, {}, set()
-    flying = [(HOP, k, node) for k, node in enumerate(flying)]
+    clock, free, done, sent = 0.0, {}, set(), []
+    flying = [(node.kb / 200, k, node) for k, node in enumerate(flying)]
     waiting = list(nodes)
     count = len(flying)
     while waiting or flying:
@@ -50,7 +54,8 @@
                 rate = PER_KB_SIBLING if link == "c" else PER_KB
                 free[link] = max(clock, free.get(link, 0.0)) + node.kb * rate * hops
                 end = max(end, free[link])
-            flying.append((end + HOP + 0.4 * (node.hops - 1), count, node))
+            flying.append((end + HOP + FURTHER * (node.hops - 1), count, node))
+            sent.append((end + HOP, node))
             count += 1
             clock += STEP
             waiting.remove(node)
@@ -58,6 +63,9 @@
         tasks = [n for n in ready if n.copy is None]
         soonest = min(flying) if flying else None
         if soonest and (soonest[0] <= clock or not tasks):
+            while sent and clock + 0.3 < soonest[0] and sent[0][0] + 1.0 < clock:
+                sent.pop(0)[1].copy.wait_send()
+                clock += 0.02
             flying.remove(soonest)
             (soonest[2].copy.wait_recv if soonest[2].links else soonest[2].copy.wait)()
             clock = max(clock, soonest[0]) + STEP
@@ -68,6 +76,8 @@
         clock += node.cost
         done.add(id(node))
         waiting.remove(node)
+    for _, node in sent:
+        node.copy.wait_send()
 
 
 def across(column):
@@ -112,11 +122,15 @@
     ):
         copy = pltpu.make_async_copy(src, dst, ls.at[len(loads)])
         copy.start()
-        loads.append(Node([], copy=copy))
+        loads.append(Node([], copy=copy, kb=src.size / 512))
     got_l, got_f, got_e, got_a, got_c = loads
 
     barrier = pltpu.get_barrier_semaphore()
-    peers = [*y_peer.values(), *x_peer.values(), z_up, z_down, z_far, *zc_peer.values()]
+    z_skip = {d: device(dz=d) for d in (2, 6)}
+    peers = [
+        z_far, *(y_peer[d] for d in (4, 3, 5, 2, 6)), *(zc_peer[i] for i in range(7, 0, -1)),
+        *z_skip.values(), x_peer[2], z_up, z_down, y_up, y_down, x_up, x_down,
+    ]
     for peer in peers:
         pl.semaphore_signal(barrier, inc=1, device_id=peer, device_id_type=MESH)
     pl.semaphore_wait(barrier, len(peers))
@@ -147,34 +161,44 @@
     def far_x(d):
         return {1: XU, 3: XD, 2: (("x+", 1), ("x-", 1))}[d]
 
-    fx = {0: got_f}
-    fx[1] = send(fbuf.at[0, 0, 0], fbuf.at[1, 0, 0], x_up, XU, 32, [got_f])
-    fx[3] = send(fbuf.at[0, 0, 0], fbuf.at[3, 0, 0], x_down, XD, 32, [got_f])
-    half_a, half_b = pl.ds(0, FW // 2), pl.ds(FW // 2, FW // 2)
-    fx2 = [
-        send(fbuf.at[1, 0, 0, :, half_a], fbuf.at[2, 0, 0, :, half_a], x_up, XU, 16, [fx[1]]),
-        send(fbuf.at[3, 0, 0, :, half_b], fbuf.at[2, 0, 0, :, half_b], x_down, XD, 16, [fx[3]]),
+    fcols = [pl.ds(h * FW // FH, FW // FH) for h in range(FH)]
+    fkb = 32 // FH
+    fz = {}
+
+    def send_fx(h):
+        own = fbuf.at[0, 0, 0, :, fcols[h]]
+        fz[0, 0, h] = [got_f]
+        for dx in (2, 1, 3):
+            fz[dx, 0, h] = [
+                send(own, fbuf.at[dx, 0, 0, :, fcols[h]], x_peer[dx], far_x(dx), fkb, [got_f], hops=2 - dx % 2, rank=0.1 * h)
+            ]
+
+    for h in range(FH):
+        send_fx(h)
+
+    lz = {0: [got_l]}
+    own = lbuf.at[0, 0, 0]
+    first, second = pl.ds(0, EW // 2), pl.ds(EW // 2, EW // 2)
+    lz[2] = [send(own, lbuf.at[0, 0, 2], z_skip[2], (("z+", 2),), 40, [got_l], hops=2)]
+    lz[6] = [send(own, lbuf.at[0, 0, 6], z_skip[6], (("z-", 2),), 40, [got_l], hops=2)]
+    lz[1] = [send(own, lbuf.at[0, 0, 1], z_up, ZU, 40, [got_l])]
+    lz[7] = [send(own, lbuf.at[0, 0, 7], z_down, ZD, 40, [got_l])]
+    lz[4] = [
+        send(lbuf.at[0, 0, 2, :, first], lbuf.at[0, 0, 4, :, first], z_skip[2], (("z+", 2),), 20, lz[2], hops=2),
+        send(lbuf.at[0, 0, 6, :, second], lbuf.at[0, 0, 4, :, second], z_skip[6], (("z-", 2),), 20, lz[6], hops=2),
     ]
-
-    lz = {0: [got_l]}
-    for k in range(1, 4):
-        lz[k] = [send(lbuf.at[0, 0, k - 1], lbuf.at[0, 0, k], z_up, ZU, 40, lz[k - 1])]
-        lz[8 - k] = [send(lbuf.at[0, 0, (9 - k) % 8], lbuf.at[0, 0, 8 - k], z_down, ZD, 40, lz[(9 - k) % 8])]
-    first, second = pl.ds(0, EW // 2), pl.ds(EW // 2, EW // 2)
-    lz[4] = [
-        send(lbuf.at[0, 0, 3, :, first], lbuf.at[0, 0, 4, :, first], z_up, ZU, 20, lz[3]),
-        send(lbuf.at[0, 0, 5, :, second], lbuf.at[0, 0, 4, :, second], z_down, ZD, 20, lz[5]),
-    ]
-
-    half = [pl.ds(0, 32), pl.ds(32, 32)]
-    e = {(0, 0): [got_e], (0, 1): [got_e]}
+    lz[3] = [send(lbuf.at[0, 0, 2], lbuf.at[0, 0, 3], z_up, ZU, 40, lz[2])]
+    lz[5] = [send(lbuf.at[0, 0, 6], lbuf.at[0, 0, 5], z_down, ZD, 40, lz[6])]
+
+    half = [pl.ds(p * 64 // EP, 64 // EP) for p in range(EP)]
+    e = {(0, p): [got_e] for p in range(EP)}
     for k in range(1, 5):
-        for p in range(2):
+        for p in range(EP):
             up, down = (k - 1, p), ((9 - k) % 8, p)
-            if k < 4 or p == 0:
-                e[k, p] = [send(ebuf.at[POS[up[0]], half[p]], ebuf.at[POS[k], half[p]], y_up, YU, 80, e[up])]
-            if k < 4 or p == 1:
-                e[8 - k, p] = [send(ebuf.at[POS[down[0]], half[p]], ebuf.at[POS[8 - k], half[p]], y_down, YD, 80, e[down])]
+            if k < 4 or p < EP // 2:
+                e[k, p] = [send(ebuf.at[POS[up[0]], half[p]], ebuf.at[POS[k], half[p]], y_up, YU, 160 // EP, e[up])]
+            if k < 4 or p >= EP // 2:
+                e[8 - k, p] = [send(ebuf.at[POS[down[0]], half[p]], ebuf.at[POS[8 - k], half[p]], y_down, YD, 160 // EP, e[down])]
 
     lx = {}
     for dz in (0, 1, 7, 2, 6, 3, 5, 4):
@@ -182,21 +206,25 @@
         lx[1, dz] = [send(lbuf.at[0, 0, dz], lbuf.at[1, 0, dz], x_up, XU, 40, lz[dz])]
         lx[3, dz] = [send(lbuf.at[0, 0, dz], lbuf.at[3, 0, dz], x_down, XD, 40, lz[dz])]
     for dz in (0, 1, 7, 2, 6, 3, 5, 4):
-        if dz < 4:
+        if dz in LXU:
+            lx[2, dz] = [send(lbuf.at[0, 0, dz], lbuf.at[2, 0, dz], x_peer[2], far_x(2), 40, lz[dz], hops=2)]
+        elif dz < 4:
             lx[2, dz] = [send(lbuf.at[1, 0, dz], lbuf.at[2, 0, dz], x_up, XU, 40, lx[1, dz])]
         else:
             lx[2, dz] = [send(lbuf.at[3, 0, dz], lbuf.at[2, 0, dz], x_down, XD, 40, lx[3, dz])]
 
-    fz = {(0, 0): [got_f], (1, 0): [fx[1]], (3, 0): [fx[3]], (2, 0): fx2}
-    for k in range(1, 4):
-        for dx in (0, 1, 3, 2):
-            up, down = (dx, k - 1), (dx, (9 - k) % 8)
-            fz[dx, k] = [send(fbuf.at[dx, 0, up[1]], fbuf.at[dx, 0, k], z_up, ZU, 32, fz[up], rank=0.1)]
-            fz[dx, 8 - k] = [send(fbuf.at[dx, 0, down[1]], fbuf.at[dx, 0, 8 - k], z_down, ZD, 32, fz[down], rank=0.1)]
-    for dx in (0, 1):
-        fz[dx, 4] = [send(fbuf.at[dx, 0, 3], fbuf.at[dx, 0, 4], z_up, ZU, 32, fz[dx, 3], rank=0.1)]
-    for dx in (3, 2):
-        fz[dx, 4] = [send(fbuf.at[dx, 0, 5], fbuf.at[dx, 0, 4], z_down, ZD, 32, fz[dx, 5], rank=0.1)]
+    def fpiece(dx, dz, h):
+        return fbuf.at[dx, 0, dz, :, fcols[h]]
+
+    for h in range(FH):
+        rank = 0.1 + 0.1 * h
+        for k in range(1, 5):
+            for dx in (0, 1, 3, 2):
+                up, down = (dx, k - 1, h), (dx, (9 - k) % 8, h)
+                if k < 4 or dx < 2:
+                    fz[dx, k, h] = [send(fpiece(*up), fpiece(dx, k, h), z_up, ZU, fkb, fz[up], rank=rank)]
+                if k < 4 or dx >= 2:
+                    fz[dx, 8 - k, h] = [send(fpiece(*down), fpiece(dx, 8 - k, h), z_down, ZD, fkb, fz[down], rank=rank)]
 
     lsib = {}
     for dx in range(4):
@@ -207,10 +235,13 @@
             )
             for p in range(2)
         ]
-    fsib = [
-        send(fbuf.at[:, 0, k], fbuf.at[:, 1, k], sibling, SC, 128, [n for dx in range(4) for n in fz[dx, k]])
-        for k in range(8)
-    ]
+    fsib = {
+        (k, h): send(
+            fbuf.at[:, 0, k, :, fcols[h]], fbuf.at[:, 1, k, :, fcols[h]], sibling, SC, 4 * fkb,
+            [n for dx in range(4) for n in fz[dx, k, h]],
+        )
+        for h in range(FH) for k in range(8)
+    }
 
     def targets(a):
         to = (a >> 3) & 63
@@ -268,7 +299,7 @@
     places = {pos: j for j, pos in POS.items()}
 
     def e_group(g):
-        return [n for j in (places[2 * g], places[2 * g + 1]) for p in range(2) for n in e[j, p]]
+        return [n for j in (places[2 * g], places[2 * g + 1]) for p in range(EP) for n in e[j, p]]
 
     def l_group(dx):
         return lsib[dx] + [n for dz in range(8) for n in lx[dx, dz]]
@@ -300,11 +331,14 @@
             rows = slice(g * 128, (g + 1) * 128)
             value = jnp.exp(dots * rowc[rows, :] * markc[dx] - SHARPNESS)
             kbuf[rows, dx * 256 : (dx + 1) * 256] = value.astype(BF16)
-        return task(work, 0.35, [row_done[g], mark_done[dx]], rank=3.0 + 0.1 * g)
+        return task(work, 0.18, [row_done[g], mark_done[dx]], rank=3.0 + 0.1 * g)
 
     tiles = {(g, dx): similar(g, dx) for g in range(4) for dx in range(4)}
 
-    factor_in = [*fsib, *(n for pieces in fz.values() for n in pieces)]
+    factor_in = [
+        [n for key, n in fsib.items() if key[-1] == h] + [n for key, pieces in fz.items() if key[-1] == h for n in pieces]
+        for h in range(FH)
+    ]
 
     def partial(g, q):
         def work():
@@ -314,7 +348,7 @@
                 preferred_element_type=F32,
             )
             pbuf[2 * g : 2 * g + 2, :, cols] = value.reshape(2, 64, QW).astype(BF16)
-        return task(work, 0.25, [*factor_in, *(tiles[g, dx] for dx in range(4))], rank=4.0 + g)
+        return task(work, 0.1, [*factor_in[q * FH // Q], *(tiles[g, dx] for dx in range(4))], rank=4.0 + g + 0.01 * q)
 
     parts = {(g, q): partial(g, q) for g in range(4) for q in range(Q)}
 
@@ -355,7 +389,7 @@
         chunk_in.append([finished, far])
         for piece, need in ((own, finished), (other, far)):
             chunk_in[q] += [
-                send(piece, piece, x_peer[d], far_x(d), 32, [need], hops=1 + d % 2) for d in (2, 1, 3)
+                send(piece, piece, x_peer[d], far_x(d), 32, [need], hops=2 - d % 2) for d in (2, 1, 3)
             ]
 
     step2 = []
@@ -416,8 +450,6 @@
     task(means, 0.2, [*summed, *step2, *counts_in], rank=0.7)
 
     emit(nodes, loads)
-    for copy in copies:
-        copy.wait_send()
 
 
 def local(embeddings, landmarks, factor, centroids, assignment):

time: 89 us -> 87 us (0.978)
  Pallas kernels: 85.3 us -> 83.3 us
    pallas_call x1, Pallas kernels: 85.3 us -> 83.3 us  [local(): pl.pallas_call(kernel, out_shape=(jax.ShapeDtypeStruct((512, 512), F32),...]
where the time goes in v3:
time: 87 us; the launch traced here: 86.8 us
  Pallas kernels  83.3 us (96%)
  local copies, waits for them, and re-layouts  2.89 us (3%)
    pallas_call x1, Pallas kernels, local(): pl.pallas_call(kernel, out_shape=(jax.ShapeDtypeStruct((512, 512), F32),...  83.3 us
    unnamed x4, local copies, waits for them, and re-layouts  2.89 us

profile of v3, /device:TPU:1, one launch (start us, length us, event | category | flops | bytes accessed | tf_op | source)
XLA Modules:
  0.0 86.8 jit_solution(10457001770756152417)
XLA Ops:
  0.6 83.3 %nystrom.1 = (f32[512,512]{1,0:T(8,128)}, f32[8,1024]{1,0:T(8,128)}) custom-call(bf16[64,1280]{1,0:T(8,128)(2,1)} %e_ref.1, bf16[16,1280]{1,0:T(8,128)(2,1)} %l_ref.1, bf16[16,1024]{1,0:T(8,128)(2,1)} %f_ref.1, bf16[512,1024]{1,0:T(8,128)(2,1)} %c_ref.1, s32[1,512]{1,0:T(1,128)} %bitcast.1), custom_call_target="tpu_custom_call" | custom-call | tf_op jit(solution)/shard_map/nystrom/pallas_call | solution.py:458
  83.9 0.0 copy-start
  83.9 2.3 %copy.9 = f32[512,512]{1,0:T(8,128)} copy(f32[512,512]{1,0:T(8,128)} %get-tuple-element.4) | data formatting | bytes 2097152
  86.2 0.0 copy-done
  86.2 0.6 copy.10
Async XLA Ops:
  83.9 2.3 %copy-start = (f32[8,1024]{1,0:T(8,128)S(1)}, f32[8,1024]{1,0:T(8,128)}, u32[]{:S(2)}) copy-start(f32[8,1024]{1,0:T(8,128)} %get-tuple-element.5) | copy-start | bytes 98308
